TPU v7x, 512 devices: a whole 4x4x16 slice. The times are simulated.
512 devices in a mesh: blk: 32 (over y, x, core), qsub: 16 (over z).
Axes of the slice: x: 4, y: 4, z: 16, core: 2. Of those that a mesh axis runs over, the one named last changes fastest.
Arguments:
- queries: bfloat16 [196608, 128], P(('blk', 'qsub')), may hold values from -6 to 6
- key_rows: bfloat16 [196608, 128], P('blk'), may hold values from -6 to 6
- log_norms: bfloat16 [196608], P(('blk', 'qsub')), may hold values from 8 to 12
- positions: int32 [196608], P(('blk', 'qsub')), may hold values from 0 to 12287, as said below
Outputs:
- key_score: float32 [196608], P('blk')
Inputs may be any that keep to these rules, and one draw needn't show every extreme that they name: positions is 0 at the first token of each document and rises by one per token within it; no document is longer than 12288 tokens and one is exactly 12288 long.
All inputs are finite; a program needn't handle non-finite values.
Results may differ from a plain program's by a relative error of at most 0.0003.
Values may be sent and summed in bfloat16 or wider, within the bound.
A program may use at most 64 MiB of HBM per device.

v0:
```python
import jax
import jax.numpy as jnp
from jax import lax
from jax.sharding import PartitionSpec as P

NEG = -1e30


def from_behind(array, axis, by):
    peers = lax.axis_size(axis)
    pairs = [(i, i + by) for i in range(peers) if 0 <= i + by < peers]
    return lax.ppermute(array, axis, pairs)


def from_behind_2(array, axis, by):
    peers = lax.axis_size(axis)
    return lax.ppermute(array, axis, [(i, (i + by) % peers) for i in range(peers)])


def column_max(query_rows, norm_rows, row_index, lower_index, key_block):
    total = query_rows.shape[0]
    block_rows = min(512, total)
    number = total // block_rows
    query_blocks = query_rows.reshape(number, block_rows, query_rows.shape[1])
    norm_blocks = norm_rows.astype(jnp.float32).reshape(number, block_rows)
    row_blocks = row_index.reshape(number, block_rows)
    lower_blocks = lower_index.reshape(number, block_rows)
    columns = jnp.arange(key_block.shape[0], dtype=jnp.int32)
    factor = key_block.shape[1] ** (-0.5)

    def absorb(running, pieces):
        query_piece, norm_piece, row_piece, lower_piece = pieces
        scores = lax.dot_general(
            query_piece, key_block, (((1,), (1,)), ((), ())), preferred_element_type=jnp.float32
        )
        scores = scores * factor - norm_piece[:, None]
        visible = (columns[None, :] <= row_piece[:, None]) & (
            columns[None, :] >= lower_piece[:, None]
        )
        return (
            jnp.maximum(running, jnp.max(jnp.where(visible, scores, jnp.float32(NEG)), axis=0)),
            None,
        )

    start = jnp.full((key_block.shape[0],), NEG, jnp.float32)
    running, _ = lax.scan(absorb, start, (query_blocks, norm_blocks, row_blocks, lower_blocks))
    return running


def body(queries, key_rows, log_norms, positions):
    total = queries.shape[0]
    key_count = key_rows.shape[0]
    row_index = lax.axis_index("qsub") * total + jnp.arange(total, dtype=jnp.int32)
    shifted_rows = row_index + key_count
    home_max = column_max(queries, log_norms, row_index, row_index - positions, key_rows)
    earlier = from_behind(key_rows, "blk", 1)
    partial_value = column_max(queries, log_norms, shifted_rows, shifted_rows - positions, earlier)
    reduced = lax.pmax((home_max, partial_value), "qsub")
    returned = from_behind_2(reduced[1], "blk", -1)
    return jnp.maximum(reduced[0], returned)


def solution(mesh):
    in_specs = (P(("blk", "qsub"), None), P("blk", None), P(("blk", "qsub")), P(("blk", "qsub")))
    out_specs = P("blk")
    return jax.shard_map(body, mesh=mesh, in_specs=in_specs, out_specs=out_specs, check_vma=False)
```

profile of v0, /device:TPU:1, one launch (start us, length us, event | category | flops | bytes accessed | tf_op | source)
XLA Modules:
  0.0 94.5 jit_solution(4859102505808839681)
XLA Ops:
  0.0 0.0 copy-start
  0.0 4.6 %collective-permute-start = (bf16[6144,128]{1,0:T(8,128)(2,1)}, bf16[6144,128]{1,0:T(8,128)(2,1)S(1)}, u32[]{:S(2)}, u32[]{:S(2)}) collective-permute-start(bf16[6144,128]{1,0:T(8,128)(2,1)} %param.5), channel_id=1, source_target_pairs={{0,16},{16,32},{32,48},{48,64},{64,80},{80,96},{96,112},{112,128},... | collective-permute-start | bytes 4718600 | tf_op jit(solution)/shard_map/ppermute | solution.py:12
  4.6 0.7 convert_element_type.4
  5.3 0.7 fusion.4
  6.0 0.0 copy-done
  6.0 5.0 %select_reduce_fusion.1 = f32[6144]{0:T(1024)S(1)} fusion(bf16[384,128]{1,0:T(8,128)(2,1)S(1)} %copy-done, bf16[6144,128]{1,0:T(8,128)(2,1)} %param.5, f32[384]{0:T(512)S(1)} %convert_element_type.4, s32[384]{0:T(512)S(1)} %get-tuple-element.38, s32[384]{0:T(512)S(1)} %iota_add_fusion), kind=kOutput, calls=%fused_computation.3 | convolution fusion | flops 620488704 | bytes 1700352 | tf_op jit(solution)/shard_map/while/body/eval_jaxpr/dot_general | solution.py:33
  11.0 11.3 %collective-permute-done = bf16[6144,128]{1,0:T(8,128)(2,1)S(1)} collective-permute-done((bf16[6144,128]{1,0:T(8,128)(2,1)}, bf16[6144,128]{1,0:T(8,128)(2,1)S(1)}, u32[]{:S(2)}, u32[]{:S(2)}) %collective-permute-start) | collective-permute-done | bytes 1572896 | tf_op jit(solution)/shard_map/ppermute | solution.py:12
  22.3 3.6 %select_reduce_fusion = f32[6144]{0:T(1024)S(1)} fusion(bf16[384,128]{1,0:T(8,128)(2,1)S(1)} %copy-done, bf16[6144,128]{1,0:T(8,128)(2,1)S(1)} %collective-permute-done, s32[384]{0:T(512)S(1)} %get-tuple-element.37, s32[384]{0:T(512)S(1)} %get-tuple-element.39, f32[384]{0:T(512)S(1)} %convert_element_type.4), kind=kOutput, calls=%fused_computation | convolution fusion | flops 620488704 | bytes 1700352 | tf_op jit(solution)/shard_map/while/body/eval_jaxpr/dot_general | solution.py:33
  25.9 48.1 %all-reduce = (f32[6144]{0:T(1024)S(1)}, f32[6144]{0:T(1024)S(1)}) all-reduce(f32[6144]{0:T(1024)S(1)} %broadcast_maximum_fusion.1, f32[6144]{0:T(1024)S(1)} %broadcast_maximum_fusion), channel_id=1, replica_groups=mesh['blk'=32,'qsub'=16] {'qsub'}, use_global_device_ids=true, to_apply=%region_1.2 | all-reduce | flops 12288 | bytes 98304 | tf_op jit(solution)/shard_map/pmax | solution.py:58
  74.0 3.5 %collective-permute-start.1 = (f32[6144]{0:T(1024)S(1)}, f32[6144]{0:T(1024)S(1)}, u32[]{:S(2)}, u32[]{:S(2)}) collective-permute-start(f32[6144]{0:T(1024)S(1)} %get-tuple-element.36), channel_id=1, source_target_pairs={{0,496},{16,0},{32,16},{48,32},{64,48},{80,64},{96,80},{112,96},{1... | collective-permute-start | bytes 73736 | tf_op jit(solution)/shard_map/ppermute | solution.py:17
  77.5 16.3 %collective-permute-done.1 = f32[6144]{0:T(1024)S(1)} collective-permute-done((f32[6144]{0:T(1024)S(1)}, f32[6144]{0:T(1024)S(1)}, u32[]{:S(2)}, u32[]{:S(2)}) %collective-permute-start.1) | collective-permute-done | bytes 24608 | tf_op jit(solution)/shard_map/ppermute | solution.py:17
  93.8 0.6 max.17
  (3 shorter events, 0.0 us)
Async XLA Ops:
  0.0 6.0 %copy-start = (bf16[384,128]{1,0:T(8,128)(2,1)S(1)}, bf16[384,128]{1,0:T(8,128)(2,1)}, u32[]{:S(2)}) copy-start(bf16[384,128]{1,0:T(8,128)(2,1)} %param.4) | copy-start | bytes 294916
  0.0 22.3 %collective-permute-start = (bf16[6144,128]{1,0:T(8,128)(2,1)}, bf16[6144,128]{1,0:T(8,128)(2,1)S(1)}, u32[]{:S(2)}, u32[]{:S(2)}) collective-permute-start(bf16[6144,128]{1,0:T(8,128)(2,1)} %param.5), channel_id=1, source_target_pairs={{0,16},{16,32},{32,48},{48,64},{64,80},{80,96},{96,112},{112,128},... | collective-permute-start | bytes 4718600 | tf_op jit(solution)/shard_map/ppermute | solution.py:12
  74.0 19.9 %collective-permute-start.1 = (f32[6144]{0:T(1024)S(1)}, f32[6144]{0:T(1024)S(1)}, u32[]{:S(2)}, u32[]{:S(2)}) collective-permute-start(f32[6144]{0:T(1024)S(1)} %get-tuple-element.36), channel_id=1, source_target_pairs={{0,496},{16,0},{32,16},{48,32},{64,48},{80,64},{96,80},{112,96},{1... | collective-permute-start | bytes 73736 | tf_op jit(solution)/shard_map/ppermute | solution.py:17
where the time goes:
time: 95.9 us; the launch traced here: 94.5 us
  blocking collectives  48.1 us (50%)
  waiting for transfers between devices  27.6 us (29%)
  matrix products  8.55 us (9%)
  starting transfers between devices  8.14 us (8%)
  other arithmetic  1.99 us (2%)
    pmax x1, blocking collectives, body(): reduced = lax.pmax((home_max, partial_value), 'qsub')  48.1 us
    ppermute x1, waiting for transfers between devices, from_behind_2(): lax.ppermute(array, axis, [(i, (i + by) % peers) for i in range(peers)])  16.3 us
    ppermute x1, waiting for transfers between devices, from_behind(): return lax.ppermute(array, axis, pairs)  11.3 us
    dot_general x2, matrix products, absorb(): lax.dot_general(query_piece, key_block, (((1,), (1,)), ((), ())), preferr...  8.55 us
    ppermute x1, starting transfers between devices, from_behind(): return lax.ppermute(array, axis, pairs)  4.63 us
    ppermute x1, starting transfers between devices, from_behind_2(): lax.ppermute(array, axis, [(i, (i + by) % peers) for i in range(peers)])  3.51 us
  transfers between devices with their start and end apart: 2, of which 2 were waited for; matrix products, arithmetic and copies ran while one was open for 7% of the time, Pallas kernels for 0%

commit v1 on v0

v1 whole, which is shorter than its diff:
```python
import functools

import jax
import jax.numpy as jnp
from jax import lax
from jax.experimental import pallas as pl
from jax.experimental.pallas import tpu as pltpu
from jax.sharding import PartitionSpec as P

MESH = pl.DeviceIdType.MESH
NEG = -1e30
FAR = 1e30
TILE = 256


def dot_rows(left, right):
    return lax.dot_general(left, right, (((1,), (1,)), ((), ())), preferred_element_type=jnp.float32)


def down(row):
    return jnp.transpose(jnp.broadcast_to(row, (128, row.shape[1])))


def off_diagonal(q_ref, c_ref, k_ref, first, width):
    query = q_ref[...]
    rows = query.shape[0]
    columns = c_ref[...]
    parts = []
    for tile in range(width // TILE):
        keys = k_ref[pl.ds(pl.multiple_of(first + tile * TILE, TILE), TILE), :]
        score = dot_rows(query, keys)
        score = score - jnp.concatenate([columns] * (TILE // 128), axis=1)
        parts.append(jnp.max(score, axis=0, keepdims=True))
    return jnp.concatenate(parts, axis=1)


def kernel(
    n_blk, n_z, scale,
    q_hbm, k_hbm, ln_hbm, pos_hbm, out_ref,
    q_v, k_v, ln_v, pos_v, qn_v, cs_v, cn_v, ch_col, cd_col, lo_col, cn_col,
    home_v, part_v, recv_v, own_v,
    in_sem, qs_sem, qr_sem, cs_sem, cr_sem, rs_send, rs_recv, ag_send, ag_recv, own_sem,
):
    b = lax.axis_index("blk")
    z = lax.axis_index("qsub")
    rows = q_v.shape[0]
    n_keys = k_v.shape[0]
    pair = 2 * rows
    n_pair = n_keys // pair
    before = lax.rem(b + n_blk - 1, n_blk)
    after = lax.rem(b + 1, n_blk)

    barrier = pltpu.get_barrier_semaphore()
    pl.semaphore_signal(barrier, inc=1, device_id={"blk": before}, device_id_type=MESH)
    pl.semaphore_signal(barrier, inc=1, device_id={"blk": after}, device_id_type=MESH)
    for step in range(1, n_z):
        pl.semaphore_signal(barrier, inc=1, device_id={"qsub": lax.rem(z + step, n_z)}, device_id_type=MESH)

    ins = [
        pltpu.make_async_copy(ln_hbm, ln_v, in_sem.at[0]),
        pltpu.make_async_copy(pos_hbm, pos_v, in_sem.at[1]),
        pltpu.make_async_copy(q_hbm, q_v, in_sem.at[2]),
        pltpu.make_async_copy(k_hbm, k_v, in_sem.at[3]),
    ]
    for copy in ins:
        copy.start()
    ins[0].wait()
    ins[1].wait()

    start = z * rows
    lane = lax.broadcasted_iota(jnp.int32, (1, rows), 1)
    pos = pos_v[...].reshape(1, rows)
    norm = ln_v[...].astype(jnp.float32).reshape(1, rows) * (1.0 / scale)
    first_pos = pos[:, 0:1]
    c_home = jnp.where(pos > lane, norm, FAR)
    c_next = jnp.where(pos > lane + start, norm, FAR)
    low_home = start - first_pos
    low_next = n_keys + start - first_pos
    cs_v[0:1, :] = c_next
    cs_v[1:2, :] = jnp.broadcast_to(low_next.astype(jnp.float32), (1, rows))

    pl.semaphore_wait(barrier, n_z + 1)
    send_q = pltpu.make_async_remote_copy(
        src_ref=q_hbm, dst_ref=qn_v, send_sem=qs_sem, recv_sem=qr_sem,
        device_id={"blk": before}, device_id_type=MESH)
    send_c = pltpu.make_async_remote_copy(
        src_ref=cs_v, dst_ref=cn_v, send_sem=cs_sem, recv_sem=cr_sem,
        device_id={"blk": before}, device_id_type=MESH)
    send_c.start()
    send_q.start()

    ch_col[...] = down(c_home)
    cd_col[...] = down(norm)
    lo_col[...] = down((lane - pos).astype(jnp.float32))

    home_v[...] = jnp.full(home_v.shape, NEG, jnp.float32)
    ins[2].wait()
    ins[3].wait()
    key_lane = lax.broadcasted_iota(jnp.int32, (1, pair), 1)

    def home_step(m, carry):
        best = off_diagonal(q_v, ch_col, k_v, m * pair, pair)
        j = key_lane + m * pair
        home_v[m] = jnp.where((j >= low_home) & (j < start), best, NEG)
        return carry

    lax.fori_loop(0, lax.div(z, 2) + 1, home_step, 0)

    keys = k_v[pl.ds(pl.multiple_of(start, 128), rows), :]
    score = dot_rows(q_v[...], keys)
    wide = rows // 128
    score = score - jnp.concatenate([cd_col[...]] * wide, axis=1)
    j = lax.broadcasted_iota(jnp.int32, (rows, rows), 1)
    r = lax.broadcasted_iota(jnp.int32, (rows, rows), 0)
    low = jnp.concatenate([lo_col[...]] * wide, axis=1)
    score = jnp.where((j <= r) & (j.astype(jnp.float32) >= low), score, NEG)
    own = jnp.max(score, axis=0, keepdims=True)
    own = jnp.concatenate([own, own], axis=1)
    mine = lax.div(z, 2)
    home_v[mine] = jnp.maximum(home_v[mine], jnp.where(lax.div(key_lane, rows) == lax.rem(z, 2), own, NEG))

    send_c.wait_recv()
    cn = cn_v[...]
    cn_col[...] = down(cn[0:1, :])
    low_n = jnp.where(b < n_blk - 1, cn[1:2, 0:1], jnp.float32(4 * n_keys)).astype(jnp.int32)
    send_q.wait_recv()

    def reduce_copy(p):
        return pltpu.make_async_remote_copy(
            src_ref=part_v.at[lax.div(p, 2), :, pl.ds(pl.multiple_of(lax.rem(p, 2) * rows, 128), rows)],
            dst_ref=recv_v.at[z], send_sem=rs_send.at[p], recv_sem=rs_recv.at[z],
            device_id={"qsub": p}, device_id_type=MESH)

    def next_step(t, carry):
        half = lax.div(t + 1, 2)
        off = n_pair // 2 + jnp.where(lax.rem(t, 2) == 0, half, -half)
        m = lax.rem(mine + off, n_pair)
        best = off_diagonal(qn_v, cn_col, k_v, m * pair, pair)
        j = key_lane + m * pair
        part_v[m] = jnp.maximum(home_v[m], jnp.where(j >= low_n, best, NEG))
        for side in range(2):
            p = 2 * m + side

            @pl.when(p != z)
            def _():
                reduce_copy(p).start()
        return carry

    lax.fori_loop(0, n_pair, next_step, 0)

    both = part_v[mine]
    recv_v[z] = jnp.where(lax.rem(z, 2) == 0, both[:, :rows], both[:, rows:])

    def wait_reduce(s, carry):
        p = lax.rem(z + s, n_z)
        pltpu.make_async_remote_copy(
            src_ref=recv_v.at[p], dst_ref=recv_v.at[p], send_sem=rs_send.at[p], recv_sem=rs_recv.at[p],
            device_id={"qsub": p}, device_id_type=MESH).wait_recv()
        return carry

    lax.fori_loop(1, n_z, wait_reduce, 0)
    own_v[...] = jnp.max(recv_v[...], axis=0) * scale

    def gather_copy(p):
        return pltpu.make_async_remote_copy(
            src_ref=own_v, dst_ref=out_ref.at[z], send_sem=ag_send.at[p], recv_sem=ag_recv.at[z],
            device_id={"qsub": p}, device_id_type=MESH)

    def gather_start(s, carry):
        gather_copy(lax.rem(z + s, n_z)).start()
        return carry

    lax.fori_loop(1, n_z, gather_start, 0)
    keep = pltpu.make_async_copy(own_v, out_ref.at[z], own_sem)
    keep.start()

    def finish(s, carry):
        p = lax.rem(z + s, n_z)
        pltpu.make_async_remote_copy(
            src_ref=own_v, dst_ref=out_ref.at[p], send_sem=ag_send.at[p], recv_sem=ag_recv.at[p],
            device_id={"qsub": p}, device_id_type=MESH).wait()
        reduce_copy(p).wait_send()
        return carry

    lax.fori_loop(1, n_z, finish, 0)
    send_q.wait_send()
    send_c.wait_send()
    keep.wait()


def solution(mesh):
    n_blk, n_z = mesh.shape["blk"], mesh.shape["qsub"]

    def body(queries, key_rows, log_norms, positions):
        rows, head = queries.shape
        n_keys = key_rows.shape[0]
        pair = 2 * rows
        f32 = jnp.float32
        dma = pltpu.SemaphoreType.DMA
        out = pl.pallas_call(
            functools.partial(kernel, n_blk, n_z, head ** -0.5),
            out_shape=jax.ShapeDtypeStruct((n_z, 1, rows), f32),
            in_specs=[pl.BlockSpec(memory_space=pl.ANY)] * 4,
            out_specs=pl.BlockSpec(memory_space=pl.ANY),
            scratch_shapes=[
                pltpu.VMEM((rows, head), jnp.bfloat16),
                pltpu.VMEM((n_keys, head), jnp.bfloat16),
                pltpu.VMEM((rows,), jnp.bfloat16),
                pltpu.VMEM((rows,), jnp.int32),
                pltpu.VMEM((rows, head), jnp.bfloat16),
                pltpu.VMEM((2, rows), f32),
                pltpu.VMEM((2, rows), f32),
                pltpu.VMEM((rows, 128), f32),
                pltpu.VMEM((rows, 128), f32),
                pltpu.VMEM((rows, 128), f32),
                pltpu.VMEM((rows, 128), f32),
                pltpu.VMEM((n_keys // pair, 1, pair), f32),
                pltpu.VMEM((n_keys // pair, 1, pair), f32),
                pltpu.VMEM((n_z, 1, rows), f32),
                pltpu.VMEM((1, rows), f32),
                dma((4,)), dma, dma, dma, dma,
                dma((n_z,)), dma((n_z,)), dma((n_z,)), dma((n_z,)), dma,
            ],
            compiler_params=pltpu.CompilerParams(collective_id=0, has_side_effects=True),
        )(queries, key_rows, log_norms, positions)
        return out.reshape(n_keys)

    in_specs = (P(("blk", "qsub"), None), P("blk", None), P(("blk", "qsub")), P(("blk", "qsub")))
    return jax.shard_map(body, mesh=mesh, in_specs=in_specs, out_specs=P("blk"), check_vma=False)
```

time: 95.9 us -> 34.7 us (0.36); the launches traced: 94.5 us -> 34.5 us
  blocking collectives: 48.1 us -> 0 us
  Pallas kernels: 0 us -> 33.2 us
  waiting for transfers between devices: 27.6 us -> 0 us
  matrix products: 8.55 us -> 0 us
  starting transfers between devices: 8.14 us -> 0 us
  other arithmetic: 1.99 us -> 0 us
  local copies, waits for them, and re-layouts: 0.01 us -> 1.35 us
    pmax x1 -> x0, blocking collectives: 48.1 us -> none  [body(): reduced = lax.pmax((home_max, partial_value), 'qsub')]
    pallas_call x0 -> x1, Pallas kernels: none -> 33.2 us  [body(): pl.pallas_call(functools.partial(kernel, n_blk, n_z, head ** (-0.5)), out...]
    ppermute x2 -> x0, waiting for transfers between devices: 27.6 us -> none  [the longest x1 16.3 us: from_behind_2(): lax.ppermute(array, axis, [(i, (i + by) % peers) for i in range(peers)])]
    dot_general x2 -> x0, matrix products: 8.55 us -> none  [absorb(): lax.dot_general(query_piece, key_block, (((1,), (1,)), ((), ())), preferr...]
    ppermute x2 -> x0, starting transfers between devices: 8.14 us -> none  [the longest x1 4.63 us: from_behind(): return lax.ppermute(array, axis, pairs)]
    unnamed x2 -> x1, local copies, waits for them, and re-layouts: 0.01 us -> 1.35 us
  transfers between devices with their start and end apart: 2 -> 0, of which waited for: 2 -> 0; matrix products, arithmetic and copies ran while one was open for 7% -> 0% of each run, Pallas kernels for 0% -> 0%
where the time goes in v1:
time: 34.7 us; the launch traced here: 34.5 us
  Pallas kernels  33.2 us (96%)
  local copies, waits for them, and re-layouts  1.35 us (4%)
    pallas_call x1, Pallas kernels, body(): pl.pallas_call(functools.partial(kernel, n_blk, n_z, head ** (-0.5)), out...  33.2 us
    unnamed x1, local copies, waits for them, and re-layouts  1.35 us

profile of v1, /device:TPU:1, one launch (start us, length us, event | category | flops | bytes accessed | tf_op | source)
XLA Modules:
  0.0 34.5 jit_solution(15218703297253173829)
XLA Ops:
  0.0 33.2 %shard_map.46 = f32[16,1,384]{2,1,0:T(1,128)} custom-call(bf16[384,128]{1,0:T(8,128)(2,1)} %q_hbm.1, bf16[6144,128]{1,0:T(8,128)(2,1)} %k_hbm.1, bf16[384]{0:T(512)(128)(2,1)} %ln_hbm.1, s32[384]{0:T(512)} %pos_hbm.1), custom_call_target="tpu_custom_call" | custom-call | tf_op jit(solution)/shard_map/pallas_call | solution.py:200
  33.2 1.3 %copy.6 = f32[6144]{0:T(1024)} copy(f32[6144]{0:T(1024)} %bitcast.1) | data formatting | bytes 49152

commit v2 on v1

--- a/solution.py
+++ b/solution.py
@@ -35,11 +35,11 @@
 
 
 def kernel(
-    n_blk, n_z, scale,
+    n_blk, n_z, near, scale,
     q_hbm, k_hbm, ln_hbm, pos_hbm, out_ref,
     q_v, k_v, ln_v, pos_v, qn_v, cs_v, cn_v, ch_col, cd_col, lo_col, cn_col,
-    home_v, part_v, recv_v, own_v,
-    in_sem, qs_sem, qr_sem, cs_sem, cr_sem, rs_send, rs_recv, ag_send, ag_recv, own_sem,
+    home_v, part_v, recv_v, full_v,
+    in_sem, qs_sem, qr_sem, cs_sem, cr_sem, rs_send, rs_recv, near_send, near_recv, far_send, far_recv, own_sem,
 ):
     b = lax.axis_index("blk")
     z = lax.axis_index("qsub")
@@ -51,10 +51,12 @@
     after = lax.rem(b + 1, n_blk)
 
     barrier = pltpu.get_barrier_semaphore()
-    pl.semaphore_signal(barrier, inc=1, device_id={"blk": before}, device_id_type=MESH)
     pl.semaphore_signal(barrier, inc=1, device_id={"blk": after}, device_id_type=MESH)
-    for step in range(1, n_z):
-        pl.semaphore_signal(barrier, inc=1, device_id={"qsub": lax.rem(z + step, n_z)}, device_id_type=MESH)
+
+    @pl.when(z == 0)
+    def _():
+        for p in range(1, n_z):
+            pl.semaphore_signal(barrier, inc=1, device_id={"qsub": p}, device_id_type=MESH)
 
     ins = [
         pltpu.make_async_copy(ln_hbm, ln_v, in_sem.at[0]),
@@ -79,7 +81,14 @@
     cs_v[0:1, :] = c_next
     cs_v[1:2, :] = jnp.broadcast_to(low_next.astype(jnp.float32), (1, rows))
 
-    pl.semaphore_wait(barrier, n_z + 1)
+    @pl.when(z == 0)
+    def _():
+        pl.semaphore_wait(barrier, 1)
+
+    @pl.when(z != 0)
+    def _():
+        pl.semaphore_wait(barrier, 2)
+
     send_q = pltpu.make_async_remote_copy(
         src_ref=q_hbm, dst_ref=qn_v, send_sem=qs_sem, recv_sem=qr_sem,
         device_id={"blk": before}, device_id_type=MESH)
@@ -125,67 +134,87 @@
     low_n = jnp.where(b < n_blk - 1, cn[1:2, 0:1], jnp.float32(4 * n_keys)).astype(jnp.int32)
     send_q.wait_recv()
 
-    def reduce_copy(p):
+    def reduce_copy(m):
         return pltpu.make_async_remote_copy(
-            src_ref=part_v.at[lax.div(p, 2), :, pl.ds(pl.multiple_of(lax.rem(p, 2) * rows, 128), rows)],
-            dst_ref=recv_v.at[z], send_sem=rs_send.at[p], recv_sem=rs_recv.at[z],
+            src_ref=part_v.at[m], dst_ref=recv_v.at[m, z], send_sem=rs_send.at[m], recv_sem=rs_recv.at[m],
+            device_id={"qsub": 0}, device_id_type=MESH)
+
+    def near_copy(m, p):
+        return pltpu.make_async_remote_copy(
+            src_ref=full_v.at[m], dst_ref=out_ref.at[m], send_sem=near_send.at[m, p], recv_sem=near_recv.at[m],
             device_id={"qsub": p}, device_id_type=MESH)
 
-    def next_step(t, carry):
-        half = lax.div(t + 1, 2)
-        off = n_pair // 2 + jnp.where(lax.rem(t, 2) == 0, half, -half)
-        m = lax.rem(mine + off, n_pair)
+    def far_copy(p):
+        return pltpu.make_async_remote_copy(
+            src_ref=full_v, dst_ref=out_ref, send_sem=far_send.at[p], recv_sem=far_recv,
+            device_id={"qsub": p}, device_id_type=MESH)
+
+    def next_step(m, carry):
         best = off_diagonal(qn_v, cn_col, k_v, m * pair, pair)
         j = key_lane + m * pair
-        part_v[m] = jnp.maximum(home_v[m], jnp.where(j >= low_n, best, NEG))
-        for side in range(2):
-            p = 2 * m + side
-
-            @pl.when(p != z)
-            def _():
-                reduce_copy(p).start()
+        part = jnp.maximum(home_v[m], jnp.where(j >= low_n, best, NEG))
+
+        @pl.when(z == 0)
+        def _():
+            recv_v[m, 0] = part
+
+        @pl.when(z != 0)
+        def _():
+            part_v[m] = part
+            reduce_copy(m).start()
+
         return carry
 
     lax.fori_loop(0, n_pair, next_step, 0)
 
-    both = part_v[mine]
-    recv_v[z] = jnp.where(lax.rem(z, 2) == 0, both[:, :rows], both[:, rows:])
-
-    def wait_reduce(s, carry):
-        p = lax.rem(z + s, n_z)
-        pltpu.make_async_remote_copy(
-            src_ref=recv_v.at[p], dst_ref=recv_v.at[p], send_sem=rs_send.at[p], recv_sem=rs_recv.at[p],
-            device_id={"qsub": p}, device_id_type=MESH).wait_recv()
-        return carry
-
-    lax.fori_loop(1, n_z, wait_reduce, 0)
-    own_v[...] = jnp.max(recv_v[...], axis=0) * scale
-
-    def gather_copy(p):
-        return pltpu.make_async_remote_copy(
-            src_ref=own_v, dst_ref=out_ref.at[z], send_sem=ag_send.at[p], recv_sem=ag_recv.at[z],
-            device_id={"qsub": p}, device_id_type=MESH)
-
-    def gather_start(s, carry):
-        gather_copy(lax.rem(z + s, n_z)).start()
-        return carry
-
-    lax.fori_loop(1, n_z, gather_start, 0)
-    keep = pltpu.make_async_copy(own_v, out_ref.at[z], own_sem)
-    keep.start()
-
-    def finish(s, carry):
-        p = lax.rem(z + s, n_z)
-        pltpu.make_async_remote_copy(
-            src_ref=own_v, dst_ref=out_ref.at[p], send_sem=ag_send.at[p], recv_sem=ag_recv.at[p],
-            device_id={"qsub": p}, device_id_type=MESH).wait()
-        reduce_copy(p).wait_send()
-        return carry
-
-    lax.fori_loop(1, n_z, finish, 0)
+    @pl.when(z == 0)
+    def _():
+        def collect(m, carry):
+            arrived = recv_v.at[m, pl.ds(1, n_z - 1)]
+            pltpu.make_async_copy(arrived, arrived, rs_recv.at[m]).wait()
+            full_v[m] = jnp.max(recv_v[m], axis=0) * scale
+            for p in range(1, near + 1):
+                near_copy(m, p).start()
+            return carry
+
+        lax.fori_loop(0, n_pair, collect, 0)
+        keep = pltpu.make_async_copy(full_v, out_ref, own_sem)
+        keep.start()
+        for p in range(near + 1, n_z):
+            far_copy(p).start()
+        keep.wait()
+
+        def drain(m, carry):
+            for p in range(1, near + 1):
+                near_copy(m, p).wait_send()
+            return carry
+
+        lax.fori_loop(0, n_pair, drain, 0)
+        for p in range(near + 1, n_z):
+            far_copy(p).wait_send()
+
+    @pl.when(z != 0)
+    def _():
+        def drain(m, carry):
+            reduce_copy(m).wait_send()
+            return carry
+
+        lax.fori_loop(0, n_pair, drain, 0)
+
+        @pl.when(z <= near)
+        def _():
+            def arrive(m, carry):
+                near_copy(m, 0).wait_recv()
+                return carry
+
+            lax.fori_loop(0, n_pair, arrive, 0)
+
+        @pl.when(z > near)
+        def _():
+            far_copy(0).wait_recv()
+
     send_q.wait_send()
     send_c.wait_send()
-    keep.wait()
 
 
 def solution(mesh):
@@ -198,8 +227,8 @@
         f32 = jnp.float32
         dma = pltpu.SemaphoreType.DMA
         out = pl.pallas_call(
-            functools.partial(kernel, n_blk, n_z, head ** -0.5),
-            out_shape=jax.ShapeDtypeStruct((n_z, 1, rows), f32),
+            functools.partial(kernel, n_blk, n_z, min(4, n_z - 1), head ** -0.5),
+            out_shape=jax.ShapeDtypeStruct((n_keys // pair, 1, pair), f32),
             in_specs=[pl.BlockSpec(memory_space=pl.ANY)] * 4,
             out_specs=pl.BlockSpec(memory_space=pl.ANY),
             scratch_shapes=[
@@ -216,10 +245,12 @@
                 pltpu.VMEM((rows, 128), f32),
                 pltpu.VMEM((n_keys // pair, 1, pair), f32),
                 pltpu.VMEM((n_keys // pair, 1, pair), f32),
-                pltpu.VMEM((n_z, 1, rows), f32),
-                pltpu.VMEM((1, rows), f32),
+                pltpu.VMEM((n_keys // pair, n_z, 1, pair), f32),
+                pltpu.VMEM((n_keys // pair, 1, pair), f32),
                 dma((4,)), dma, dma, dma, dma,
-                dma((n_z,)), dma((n_z,)), dma((n_z,)), dma((n_z,)), dma,
+                dma((n_keys // pair,)), dma((n_keys // pair,)),
+                dma((n_keys // pair, min(4, n_z - 1) + 1)), dma((n_keys // pair,)),
+                dma((n_z,)), dma, dma,
             ],
             compiler_params=pltpu.CompilerParams(collective_id=0, has_side_effects=True),
         )(queries, key_rows, log_norms, positions)

time: 34.7 us -> 30.3 us (0.87)
  the two profiles are of different devices: /device:TPU:1 before, /device:TPU:31 now
where the time goes in v2:
time: 30.3 us; the launch traced here: 30.1 us
  Pallas kernels  28.8 us (95%)
  local copies, waits for them, and re-layouts  1.35 us (4%)
    pallas_call x1, Pallas kernels, body(): pl.pallas_call(functools.partial(kernel, n_blk, n_z, min(4, n_z - 1), hea...  28.8 us
    unnamed x1, local copies, waits for them, and re-layouts  1.35 us

profile of v2, /device:TPU:31, one launch (start us, length us, event | category | flops | bytes accessed | tf_op | source)
XLA Modules:
  0.0 30.1 jit_solution(16667892725357775674)
XLA Ops:
  0.0 28.8 %shard_map.46 = f32[8,1,768]{2,1,0:T(1,128)} custom-call(bf16[384,128]{1,0:T(8,128)(2,1)} %q_hbm.1, bf16[6144,128]{1,0:T(8,128)(2,1)} %k_hbm.1, bf16[384]{0:T(512)(128)(2,1)} %ln_hbm.1, s32[384]{0:T(512)} %pos_hbm.1), custom_call_target="tpu_custom_call" | custom-call | tf_op jit(solution)/shard_map/pallas_call | solution.py:229
  28.8 1.3 %copy.6 = f32[6144]{0:T(1024)} copy(f32[6144]{0:T(1024)} %bitcast.1) | data formatting | bytes 49152

commit v3 on v1

v3 whole, which is shorter than its diff:
```python
import functools

import jax
import jax.numpy as jnp
from jax import lax
from jax.experimental import pallas as pl
from jax.experimental.pallas import tpu as pltpu
from jax.sharding import PartitionSpec as P

MESH = pl.DeviceIdType.MESH
NEG = -1e30
FAR = 1e30
TILE = 256
HALVES = 2
PIECES = 2


def plan(n_z):
    if n_z == 16:
        return {0: [1, 2, 3, 4, 15], 3: [5], 4: [7, 6], 15: [8, 9, 10, 11, 12, 13, 14]}, 4
    return {0: list(range(1, n_z))}, 1


def dot_rows(left, right):
    return lax.dot_general(left, right, (((1,), (1,)), ((), ())), preferred_element_type=jnp.float32)


def down(row):
    return jnp.transpose(jnp.broadcast_to(row, (128, row.shape[1])))


def best_of(query, columns, k_ref, first, width):
    parts = []
    for at in range(first, first + width, TILE):
        score = dot_rows(query, k_ref[at : at + TILE, :])
        score = score - jnp.concatenate([columns] * (TILE // 128), axis=1)
        parts.append(jnp.max(score, axis=0, keepdims=True))
    return jnp.concatenate(parts, axis=1)


def kernel(
    n_blk, n_z, scale,
    q_hbm, k_hbm, ln_hbm, pos_hbm, out_ref,
    q_v, k_v, ln_v, pos_v, qn_v, cs_v, cn_v,
    home_v, part_v, recv_v, mid_v, full_v,
    in_sem, qs_sem, qr_sem, cs_sem, cr_sem, rs_send, rs_early, rs_late, ag_send, ag_recv, own_sem,
):
    b = lax.axis_index("blk")
    z = lax.axis_index("qsub")
    sends, n_late = plan(n_z)
    rows = q_v.shape[0]
    n_keys = k_v.shape[0]
    width = n_keys // PIECES
    part_rows = rows // HALVES
    before = lax.rem(b + n_blk - 1, n_blk)
    after = lax.rem(b + 1, n_blk)
    has_before = b > 0
    has_after = b < n_blk - 1
    turn = n_z // 2 - n_late
    slot = lax.rem(z + turn, n_z)
    first_late = n_z - n_late

    barrier = pltpu.get_barrier_semaphore()

    @pl.when(has_after)
    def _():
        pl.semaphore_signal(barrier, inc=1, device_id={"blk": after}, device_id_type=MESH)

    @pl.when(z == 0)
    def _():
        for p in range(1, n_z):
            pl.semaphore_signal(barrier, inc=1, device_id={"qsub": p}, device_id_type=MESH)

    ins = [
        pltpu.make_async_copy(ln_hbm, ln_v, in_sem.at[0]),
        pltpu.make_async_copy(pos_hbm, pos_v, in_sem.at[1]),
        pltpu.make_async_copy(q_hbm, q_v, in_sem.at[2]),
        pltpu.make_async_copy(k_hbm, k_v, in_sem.at[3]),
    ]
    for copy in ins:
        copy.start()
    ins[0].wait()
    ins[1].wait()

    start = z * rows
    lane = lax.broadcasted_iota(jnp.int32, (1, rows), 1)
    pos = pos_v[...].reshape(1, rows)
    norm = ln_v[...].astype(jnp.float32).reshape(1, rows) * (1.0 / scale)
    first_pos = pos[:, 0:1]
    c_home = jnp.where(pos > lane, norm, FAR)
    c_next = jnp.where(pos > lane + start, norm, FAR)
    low_home = start - first_pos
    low_next = n_keys + start - first_pos
    cs_v[0:1, :] = c_next
    cs_v[1:2, :] = jnp.broadcast_to(low_next.astype(jnp.float32), (1, rows))
    ins[2].wait()

    @pl.when(has_before & (z == 0))
    def _():
        pl.semaphore_wait(barrier, 1)

    @pl.when(has_before & (z != 0))
    def _():
        pl.semaphore_wait(barrier, 2)

    send_c = pltpu.make_async_remote_copy(
        src_ref=cs_v, dst_ref=cn_v, send_sem=cs_sem, recv_sem=cr_sem,
        device_id={"blk": before}, device_id_type=MESH)
    send_q = []
    for h in range(HALVES):
        piece = pl.ds(h * part_rows, part_rows)
        send_q.append(pltpu.make_async_remote_copy(
            src_ref=q_v.at[piece], dst_ref=qn_v.at[piece], send_sem=qs_sem.at[h], recv_sem=qr_sem.at[h],
            device_id={"blk": before}, device_id_type=MESH))

    @pl.when(has_before)
    def _():
        send_c.start()
        for copy in send_q:
            copy.start()

    home_columns = down(c_home)
    own_columns = down(norm)
    low_columns = down((lane - pos).astype(jnp.float32))

    ins[3].wait()
    query = q_v[...]
    for g in range(PIECES):
        best = best_of(query, home_columns, k_v, g * width, width)
        j = lax.broadcasted_iota(jnp.int32, (1, width), 1) + g * width
        home_v[0:1, g * width : (g + 1) * width] = jnp.where((j >= low_home) & (j < start), best, NEG)

    here = pl.ds(pl.multiple_of(start, 128), rows)
    score = dot_rows(query, k_v[here, :])
    wide = rows // 128
    score = score - jnp.concatenate([own_columns] * wide, axis=1)
    j = lax.broadcasted_iota(jnp.int32, (rows, rows), 1)
    r = lax.broadcasted_iota(jnp.int32, (rows, rows), 0)
    low = jnp.concatenate([low_columns] * wide, axis=1)
    score = jnp.where((j <= r) & (j.astype(jnp.float32) >= low), score, NEG)
    home_v[0:1, here] = jnp.maximum(home_v[0:1, here], jnp.max(score, axis=0, keepdims=True))

    @pl.when(has_after)
    def _():
        send_c.wait_recv()

    @pl.when(jnp.logical_not(has_after))
    def _():
        cn_v[...] = cs_v[...]
        qn_v[...] = q_v[...]

    cn = cn_v[...]
    next_columns = down(cn[0:1, :])
    low_n = jnp.where(has_after, cn[1:2, 0:1], jnp.float32(4 * n_keys)).astype(jnp.int32)

    def next_best(h, g):
        some = next_columns[h * part_rows : (h + 1) * part_rows, :]
        best = best_of(qn_v[h * part_rows : (h + 1) * part_rows, :], some, k_v, g * width, width)
        j = lax.broadcasted_iota(jnp.int32, (1, width), 1) + g * width
        return jnp.maximum(home_v[0:1, g * width : (g + 1) * width], jnp.where(j >= low_n, best, NEG))

    for h in range(HALVES - 1):
        @pl.when(has_after)
        def _():
            send_q[h].wait_recv()

        for g in range(PIECES):
            home_v[0:1, g * width : (g + 1) * width] = next_best(h, g)

    @pl.when(has_after)
    def _():
        send_q[HALVES - 1].wait_recv()

    def reduce_copy(g, sem):
        return pltpu.make_async_remote_copy(
            src_ref=part_v.at[g], dst_ref=recv_v.at[g, slot], send_sem=rs_send.at[g], recv_sem=sem.at[g],
            device_id={"qsub": 0}, device_id_type=MESH)

    def give(source, target, p, at, g):
        return pltpu.make_async_remote_copy(
            src_ref=source, dst_ref=target, send_sem=ag_send.at[at], recv_sem=ag_recv.at[g],
            device_id={"qsub": p}, device_id_type=MESH)

    @pl.when(z == 0)
    def _():
        for g in range(PIECES):
            recv_v[g, turn] = next_best(HALVES - 1, g)
        for g in range(PIECES):
            arrived = recv_v.at[g, pl.ds(0, first_late - 1)]
            pltpu.make_async_copy(arrived, arrived, rs_early.at[g]).wait()
            mid_v[g] = jnp.max(recv_v[g, 0:first_late], axis=0)
        given, kept = [], []
        for g in range(PIECES):
            arrived = recv_v.at[g, pl.ds(first_late, n_late)]
            pltpu.make_async_copy(arrived, arrived, rs_late.at[g]).wait()
            late = jnp.max(recv_v[g, first_late:n_z], axis=0)
            full_v[g] = jnp.maximum(mid_v[g], late) * scale
            for at, p in enumerate(sends[0]):
                given.append(give(full_v.at[g], out_ref.at[g], p, at * PIECES + g, g))
                given[-1].start()
            keep = pltpu.make_async_copy(full_v.at[g], out_ref.at[g], own_sem.at[g])
            keep.start()
            kept.append(keep)
        for copy in kept:
            copy.wait()
        for copy in given:
            copy.wait_send()

    @pl.when(z != 0)
    def _():
        @pl.when(jnp.logical_not(has_before))
        def _():
            pl.semaphore_wait(barrier, 1)

        late = (z >= n_z // 2) & (z < n_z // 2 + n_late)
        for g in range(PIECES):
            part_v[g] = next_best(HALVES - 1, g)

            @pl.when(late)
            def _():
                reduce_copy(g, rs_late).start()

            @pl.when(jnp.logical_not(late))
            def _():
                reduce_copy(g, rs_early).start()

        direct = z < 0
        for p in sends[0]:
            direct = direct | (z == p)

        @pl.when(direct)
        def _():
            for g in range(PIECES):
                give(out_ref.at[g], out_ref.at[g], 0, 0, g).wait_recv()

        @pl.when(jnp.logical_not(direct))
        def _():
            give(out_ref, out_ref, 0, 0, 0).wait_recv()

        for source, targets in sends.items():
            if source == 0:
                continue

            @pl.when(z == source)
            def _():
                given = []
                for at, p in enumerate(targets):
                    given.append(give(out_ref, out_ref, p, at, 0))
                    given[-1].start()
                for copy in given:
                    copy.wait_send()

        for g in range(PIECES):
            reduce_copy(g, rs_early).wait_send()

    @pl.when(has_before)
    def _():
        send_c.wait_send()
        for copy in send_q:
            copy.wait_send()


def solution(mesh):
    n_blk, n_z = mesh.shape["blk"], mesh.shape["qsub"]

    def body(queries, key_rows, log_norms, positions):
        rows, head = queries.shape
        n_keys = key_rows.shape[0]
        width = n_keys // PIECES
        f32 = jnp.float32
        dma = pltpu.SemaphoreType.DMA
        operands = [
            pltpu.with_memory_space_constraint(x, pltpu.HBM) for x in (queries, key_rows, log_norms, positions)
        ]
        out = pl.pallas_call(
            functools.partial(kernel, n_blk, n_z, head ** -0.5),
            out_shape=pltpu.VMEM((PIECES, 1, width), f32),
            in_specs=[pl.BlockSpec(memory_space=pl.ANY)] * 4,
            out_specs=pl.BlockSpec(memory_space=pl.ANY),
            scratch_shapes=[
                pltpu.VMEM((rows, head), jnp.bfloat16),
                pltpu.VMEM((n_keys, head), jnp.bfloat16),
                pltpu.VMEM((rows,), jnp.bfloat16),
                pltpu.VMEM((rows,), jnp.int32),
                pltpu.VMEM((rows, head), jnp.bfloat16),
                pltpu.VMEM((2, rows), f32),
                pltpu.VMEM((2, rows), f32),
                pltpu.VMEM((1, n_keys), f32),
                pltpu.VMEM((PIECES, 1, width), f32),
                pltpu.VMEM((PIECES, n_z, 1, width), f32),
                pltpu.VMEM((PIECES, 1, width), f32),
                pltpu.VMEM((PIECES, 1, width), f32),
                dma((4,)), dma((HALVES,)), dma((HALVES,)), dma, dma,
                dma((PIECES,)), dma((PIECES,)), dma((PIECES,)), dma((PIECES * n_z,)), dma((PIECES,)), dma((PIECES,)),
            ],
            compiler_params=pltpu.CompilerParams(
                collective_id=0, has_side_effects=True, vmem_limit_bytes=16 * 1024 * 1024),
        )(*operands)
        return out.reshape(n_keys)

    in_specs = (P(("blk", "qsub"), None), P("blk", None), P(("blk", "qsub")), P(("blk", "qsub")))
    return jax.shard_map(body, mesh=mesh, in_specs=in_specs, out_specs=P("blk"), check_vma=False)
```

time: 34.7 us -> 26.4 us (0.76)
  the two profiles are of different devices: /device:TPU:1 before, /device:TPU:208 now
where the time goes in v3:
time: 26.4 us; the launch traced here: 26.3 us
  Pallas kernels  25.7 us (97%)
  local copies, waits for them, and re-layouts  0.61 us (2%)
    pallas_call x1, Pallas kernels, body(): pl.pallas_call(functools.partial(kernel, n_blk, n_z, head ** (-0.5)), out...  25.7 us
    unnamed x1, local copies, waits for them, and re-layouts  0.61 us

profile of v3, /device:TPU:208, one launch (start us, length us, event | category | flops | bytes accessed | tf_op | source)
XLA Modules:
  0.0 26.3 jit_solution(14817442957295233498)
XLA Ops:
  0.0 25.7 %shard_map.46 = f32[2,1,3072]{2,1,0:T(1,128)S(1)} custom-call(bf16[384,128]{1,0:T(8,128)(2,1)} %q_hbm.1, bf16[6144,128]{1,0:T(8,128)(2,1)} %k_hbm.1, bf16[384]{0:T(512)(128)(2,1)} %ln_hbm.1, s32[384]{0:T(512)} %pos_hbm.1), custom_call_target="tpu_custom_call" | custom-call | tf_op jit(solution)/shard_map/pallas_call | solution.py:275
  25.7 0.6 %copy.6 = f32[6144]{0:T(1024)} copy(f32[6144]{0:T(1024)S(1)} %bitcast.1) | data formatting | bytes 49152

commit v4 on v3

--- a/solution.py
+++ b/solution.py
@@ -13,11 +13,12 @@
 TILE = 256
 HALVES = 2
 PIECES = 2
+STEPS = 65000.0
 
 
 def plan(n_z):
     if n_z == 16:
-        return {0: [1, 2, 3, 4, 15], 3: [5], 4: [7, 6], 15: [8, 9, 10, 11, 12, 13, 14]}, 4
+        return {0: [1, 4, 2, 5, 3, 15], 4: [6], 5: [7], 15: [8, 9, 10, 11, 12, 13, 14]}, 4
     return {0: list(range(1, n_z))}, 1
 
 
@@ -29,21 +30,65 @@
     return jnp.transpose(jnp.broadcast_to(row, (128, row.shape[1])))
 
 
+def fold(groups):
+    number = len(groups)
+    groups = groups + [groups[-1]] * (8 - number)
+    row = lax.broadcasted_iota(jnp.int32, (8, 128), 0)
+    for by in (4, 2, 1):
+        upper = (row & by) == 0
+        groups = [
+            jnp.where(
+                upper,
+                jnp.maximum(groups[i], pltpu.roll(groups[i], 8 - by, 0)),
+                jnp.maximum(groups[i + by], pltpu.roll(groups[i + by], by, 0)),
+            )
+            for i in range(by)
+        ]
+    return groups[0] if number == 8 else groups[0][:number]
+
+
+def dense(groups):
+    return jnp.concatenate([fold(groups[i : i + 8]) for i in range(0, len(groups), 8)], axis=0)
+
+
+def eighths(score):
+    rows, width = score.shape
+    best = jnp.max(score.reshape(rows // 8, 8, width), axis=0)
+    return [best[:, i : i + 128] for i in range(0, width, 128)]
+
+
 def best_of(query, columns, k_ref, first, width):
-    parts = []
+    groups = []
     for at in range(first, first + width, TILE):
         score = dot_rows(query, k_ref[at : at + TILE, :])
         score = score - jnp.concatenate([columns] * (TILE // 128), axis=1)
-        parts.append(jnp.max(score, axis=0, keepdims=True))
-    return jnp.concatenate(parts, axis=1)
+        groups += eighths(score)
+    return dense(groups)
+
+
+def key_index(g, lines):
+    line = lax.broadcasted_iota(jnp.int32, (lines, 128), 0) + g * lines
+    return line * 128 + lax.broadcasted_iota(jnp.int32, (lines, 128), 1)
+
+
+def encode(best):
+    low = jnp.min(best, axis=0, keepdims=True)
+    span = jnp.maximum(jnp.max(best, axis=0, keepdims=True) - low, 1e-6)
+    steps = jnp.round((best - low) * (STEPS / span)) - STEPS / 2
+    return steps.astype(jnp.int32).astype(jnp.int16), jnp.concatenate([low, span * (1.0 / STEPS)], axis=0)
+
+
+def decode(code, bounds):
+    steps = code.astype(jnp.int32).astype(jnp.float32) + STEPS / 2
+    return steps * bounds[1:2, :] + bounds[0:1, :]
 
 
 def kernel(
     n_blk, n_z, scale,
     q_hbm, k_hbm, ln_hbm, pos_hbm, out_ref,
     q_v, k_v, ln_v, pos_v, qn_v, cs_v, cn_v,
-    home_v, part_v, recv_v, mid_v, full_v,
-    in_sem, qs_sem, qr_sem, cs_sem, cr_sem, rs_send, rs_early, rs_late, ag_send, ag_recv, own_sem,
+    home_v, part_v, recv_v, mid_v, code_v, bound_v,
+    in_sem, qs_sem, qr_sem, cs_sem, cr_sem, rs_send, rs_early, rs_late, ag_send, ag_recv,
 ):
     b = lax.axis_index("blk")
     z = lax.axis_index("qsub")
@@ -51,6 +96,7 @@
     rows = q_v.shape[0]
     n_keys = k_v.shape[0]
     width = n_keys // PIECES
+    lines = width // 128
     part_rows = rows // HALVES
     before = lax.rem(b + n_blk - 1, n_blk)
     after = lax.rem(b + 1, n_blk)
@@ -127,8 +173,8 @@
     query = q_v[...]
     for g in range(PIECES):
         best = best_of(query, home_columns, k_v, g * width, width)
-        j = lax.broadcasted_iota(jnp.int32, (1, width), 1) + g * width
-        home_v[0:1, g * width : (g + 1) * width] = jnp.where((j >= low_home) & (j < start), best, NEG)
+        j = key_index(g, lines)
+        home_v[g * lines : (g + 1) * lines, :] = jnp.where((j >= low_home) & (j < start), best, NEG)
 
     here = pl.ds(pl.multiple_of(start, 128), rows)
     score = dot_rows(query, k_v[here, :])
@@ -138,7 +184,9 @@
     r = lax.broadcasted_iota(jnp.int32, (rows, rows), 0)
     low = jnp.concatenate([low_columns] * wide, axis=1)
     score = jnp.where((j <= r) & (j.astype(jnp.float32) >= low), score, NEG)
-    home_v[0:1, here] = jnp.maximum(home_v[0:1, here], jnp.max(score, axis=0, keepdims=True))
+    own = dense(eighths(score))
+    mine = pl.ds(z * wide, wide)
+    home_v[mine, :] = jnp.maximum(home_v[mine, :], own)
 
     @pl.when(has_after)
     def _():
@@ -156,8 +204,8 @@
     def next_best(h, g):
         some = next_columns[h * part_rows : (h + 1) * part_rows, :]
         best = best_of(qn_v[h * part_rows : (h + 1) * part_rows, :], some, k_v, g * width, width)
-        j = lax.broadcasted_iota(jnp.int32, (1, width), 1) + g * width
-        return jnp.maximum(home_v[0:1, g * width : (g + 1) * width], jnp.where(j >= low_n, best, NEG))
+        return jnp.maximum(
+            home_v[g * lines : (g + 1) * lines, :], jnp.where(key_index(g, lines) >= low_n, best, NEG))
 
     for h in range(HALVES - 1):
         @pl.when(has_after)
@@ -165,7 +213,7 @@
             send_q[h].wait_recv()
 
         for g in range(PIECES):
-            home_v[0:1, g * width : (g + 1) * width] = next_best(h, g)
+            home_v[g * lines : (g + 1) * lines, :] = next_best(h, g)
 
     @pl.when(has_after)
     def _():
@@ -176,10 +224,21 @@
             src_ref=part_v.at[g], dst_ref=recv_v.at[g, slot], send_sem=rs_send.at[g], recv_sem=sem.at[g],
             device_id={"qsub": 0}, device_id_type=MESH)
 
-    def give(source, target, p, at, g):
-        return pltpu.make_async_remote_copy(
-            src_ref=source, dst_ref=target, send_sem=ag_send.at[at], recv_sem=ag_recv.at[g],
-            device_id={"qsub": p}, device_id_type=MESH)
+    def give(p, at):
+        return [
+            pltpu.make_async_remote_copy(
+                src_ref=ref, dst_ref=ref, send_sem=ag_send.at[2 * at + i], recv_sem=ag_recv.at[i],
+                device_id={"qsub": p}, device_id_type=MESH)
+            for i, ref in enumerate((bound_v, code_v))
+        ]
+
+    def pass_on(source, done):
+        for at, p in enumerate(sends[source]):
+            for copy in give(p, at):
+                if done:
+                    copy.wait_send()
+                else:
+                    copy.start()
 
     @pl.when(z == 0)
     def _():
@@ -189,22 +248,14 @@
             arrived = recv_v.at[g, pl.ds(0, first_late - 1)]
             pltpu.make_async_copy(arrived, arrived, rs_early.at[g]).wait()
             mid_v[g] = jnp.max(recv_v[g, 0:first_late], axis=0)
-        given, kept = [], []
+        full = []
         for g in range(PIECES):
             arrived = recv_v.at[g, pl.ds(first_late, n_late)]
             pltpu.make_async_copy(arrived, arrived, rs_late.at[g]).wait()
-            late = jnp.max(recv_v[g, first_late:n_z], axis=0)
-            full_v[g] = jnp.maximum(mid_v[g], late) * scale
-            for at, p in enumerate(sends[0]):
-                given.append(give(full_v.at[g], out_ref.at[g], p, at * PIECES + g, g))
-                given[-1].start()
-            keep = pltpu.make_async_copy(full_v.at[g], out_ref.at[g], own_sem.at[g])
-            keep.start()
-            kept.append(keep)
-        for copy in kept:
-            copy.wait()
-        for copy in given:
-            copy.wait_send()
+            full.append(jnp.maximum(mid_v[g], jnp.max(recv_v[g, first_late:n_z], axis=0)) * scale)
+        code, bounds = encode(jnp.concatenate(full, axis=0))
+        code_v[...] = code
+        bound_v[...] = bounds
 
     @pl.when(z != 0)
     def _():
@@ -224,32 +275,19 @@
             def _():
                 reduce_copy(g, rs_early).start()
 
-        direct = z < 0
-        for p in sends[0]:
-            direct = direct | (z == p)
-
-        @pl.when(direct)
-        def _():
-            for g in range(PIECES):
-                give(out_ref.at[g], out_ref.at[g], 0, 0, g).wait_recv()
-
-        @pl.when(jnp.logical_not(direct))
-        def _():
-            give(out_ref, out_ref, 0, 0, 0).wait_recv()
-
-        for source, targets in sends.items():
-            if source == 0:
-                continue
-
-            @pl.when(z == source)
-            def _():
-                given = []
-                for at, p in enumerate(targets):
-                    given.append(give(out_ref, out_ref, p, at, 0))
-                    given[-1].start()
-                for copy in given:
-                    copy.wait_send()
-
+        for copy in give(0, 0):
+            copy.wait_recv()
+
+    for source in sends:
+        pl.when(z == source)(functools.partial(pass_on, source, False))
+
+    out_ref[...] = decode(code_v[...], bound_v[...])
+
+    for source in sends:
+        pl.when(z == source)(functools.partial(pass_on, source, True))
+
+    @pl.when(z != 0)
+    def _():
         for g in range(PIECES):
             reduce_copy(g, rs_early).wait_send()
 
@@ -266,7 +304,7 @@
     def body(queries, key_rows, log_norms, positions):
         rows, head = queries.shape
         n_keys = key_rows.shape[0]
-        width = n_keys // PIECES
+        lines = n_keys // PIECES // 128
         f32 = jnp.float32
         dma = pltpu.SemaphoreType.DMA
         operands = [
@@ -274,9 +312,9 @@
         ]
         out = pl.pallas_call(
             functools.partial(kernel, n_blk, n_z, head ** -0.5),
-            out_shape=pltpu.VMEM((PIECES, 1, width), f32),
+            out_shape=pltpu.VMEM((n_keys // 128, 128), f32),
             in_specs=[pl.BlockSpec(memory_space=pl.ANY)] * 4,
-            out_specs=pl.BlockSpec(memory_space=pl.ANY),
+            out_specs=pl.BlockSpec(memory_space=pltpu.VMEM),
             scratch_shapes=[
                 pltpu.VMEM((rows, head), jnp.bfloat16),
                 pltpu.VMEM((n_keys, head), jnp.bfloat16),
@@ -285,13 +323,14 @@
                 pltpu.VMEM((rows, head), jnp.bfloat16),
                 pltpu.VMEM((2, rows), f32),
                 pltpu.VMEM((2, rows), f32),
-                pltpu.VMEM((1, n_keys), f32),
-                pltpu.VMEM((PIECES, 1, width), f32),
-                pltpu.VMEM((PIECES, n_z, 1, width), f32),
-                pltpu.VMEM((PIECES, 1, width), f32),
-                pltpu.VMEM((PIECES, 1, width), f32),
+                pltpu.VMEM((n_keys // 128, 128), f32),
+                pltpu.VMEM((PIECES, lines, 128), f32),
+                pltpu.VMEM((PIECES, n_z, lines, 128), f32),
+                pltpu.VMEM((PIECES, lines, 128), f32),
+                pltpu.VMEM((n_keys // 128, 128), jnp.int16),
+                pltpu.VMEM((2, 128), f32),
                 dma((4,)), dma((HALVES,)), dma((HALVES,)), dma, dma,
-                dma((PIECES,)), dma((PIECES,)), dma((PIECES,)), dma((PIECES * n_z,)), dma((PIECES,)), dma((PIECES,)),
+                dma((PIECES,)), dma((PIECES,)), dma((PIECES,)), dma((2 * n_z,)), dma((2,)),
             ],
             compiler_params=pltpu.CompilerParams(
                 collective_id=0, has_side_effects=True, vmem_limit_bytes=16 * 1024 * 1024),

time: 26.4 us -> 25.6 us (0.970)
  the two profiles are of different devices: /device:TPU:208 before, /device:TPU:1 now
where the time goes in v4:
time: 25.6 us; the launch traced here: 25.4 us
  Pallas kernels  24.8 us (97%)
  local copies, waits for them, and re-layouts  0.61 us (2%)
    pallas_call x1, Pallas kernels, body(): pl.pallas_call(functools.partial(kernel, n_blk, n_z, head ** (-0.5)), out...  24.8 us
    unnamed x1, local copies, waits for them, and re-layouts  0.61 us

profile of v4, /device:TPU:1, one launch (start us, length us, event | category | flops | bytes accessed | tf_op | source)
XLA Modules:
  0.0 25.4 jit_solution(469230860636657658)
XLA Ops:
  0.0 24.8 %shard_map.46 = f32[48,128]{1,0:T(8,128)S(1)} custom-call(bf16[384,128]{1,0:T(8,128)(2,1)} %q_hbm.1, bf16[6144,128]{1,0:T(8,128)(2,1)} %k_hbm.1, bf16[384]{0:T(512)(128)(2,1)} %ln_hbm.1, s32[384]{0:T(512)} %pos_hbm.1), custom_call_target="tpu_custom_call" | custom-call | tf_op jit(solution)/shard_map/pallas_call | solution.py:313
  24.8 0.6 %copy.6 = f32[6144]{0:T(1024)} copy(f32[6144]{0:T(1024)S(1)} %bitcast.1) | data formatting | bytes 49152

commit v5 on v4

--- a/solution.py
+++ b/solution.py
@@ -12,13 +12,14 @@
 FAR = 1e30
 TILE = 256
 HALVES = 2
-PIECES = 2
+PIECES = 3
+ROW = 8
 STEPS = 65000.0
 
 
 def plan(n_z):
     if n_z == 16:
-        return {0: [1, 4, 2, 5, 3, 15], 4: [6], 5: [7], 15: [8, 9, 10, 11, 12, 13, 14]}, 4
+        return {0: [1, 4, 2, 15, 3], 4: [5, 6, 7], 15: [8, 9, 10, 11, 12, 13, 14]}, 4
     return {0: list(range(1, n_z))}, 1
 
 
@@ -85,9 +86,9 @@
 
 def kernel(
     n_blk, n_z, scale,
-    q_hbm, k_hbm, ln_hbm, pos_hbm, out_ref,
+    q_hbm, k_hbm, ln_hbm, pos_hbm, code_v, bound_v,
     q_v, k_v, ln_v, pos_v, qn_v, cs_v, cn_v,
-    home_v, part_v, recv_v, mid_v, code_v, bound_v,
+    home_v, part_v, recv_v, mid_v,
     in_sem, qs_sem, qr_sem, cs_sem, cr_sem, rs_send, rs_early, rs_late, ag_send, ag_recv,
 ):
     b = lax.axis_index("blk")
@@ -141,14 +142,6 @@
     cs_v[1:2, :] = jnp.broadcast_to(low_next.astype(jnp.float32), (1, rows))
     ins[2].wait()
 
-    @pl.when(has_before & (z == 0))
-    def _():
-        pl.semaphore_wait(barrier, 1)
-
-    @pl.when(has_before & (z != 0))
-    def _():
-        pl.semaphore_wait(barrier, 2)
-
     send_c = pltpu.make_async_remote_copy(
         src_ref=cs_v, dst_ref=cn_v, send_sem=cs_sem, recv_sem=cr_sem,
         device_id={"blk": before}, device_id_type=MESH)
@@ -159,11 +152,21 @@
             src_ref=q_v.at[piece], dst_ref=qn_v.at[piece], send_sem=qs_sem.at[h], recv_sem=qr_sem.at[h],
             device_id={"blk": before}, device_id_type=MESH))
 
-    @pl.when(has_before)
-    def _():
+    def send_queries():
+        @pl.when(z == 0)
+        def _():
+            pl.semaphore_wait(barrier, 1)
+
+        @pl.when(z != 0)
+        def _():
+            pl.semaphore_wait(barrier, 2)
+
         send_c.start()
         for copy in send_q:
             copy.start()
+
+    far = lax.rem(b, ROW) == 0
+    pl.when(has_before & jnp.logical_not(far))(send_queries)
 
     home_columns = down(c_home)
     own_columns = down(norm)
@@ -175,6 +178,8 @@
         best = best_of(query, home_columns, k_v, g * width, width)
         j = key_index(g, lines)
         home_v[g * lines : (g + 1) * lines, :] = jnp.where((j >= low_home) & (j < start), best, NEG)
+        if g == 0:
+            pl.when(has_before & far)(send_queries)
 
     here = pl.ds(pl.multiple_of(start, 128), rows)
     score = dot_rows(query, k_v[here, :])
@@ -281,8 +286,6 @@
     for source in sends:
         pl.when(z == source)(functools.partial(pass_on, source, False))
 
-    out_ref[...] = decode(code_v[...], bound_v[...])
-
     for source in sends:
         pl.when(z == source)(functools.partial(pass_on, source, True))
 
@@ -310,11 +313,11 @@
         operands = [
             pltpu.with_memory_space_constraint(x, pltpu.HBM) for x in (queries, key_rows, log_norms, positions)
         ]
-        out = pl.pallas_call(
+        code, bounds = pl.pallas_call(
             functools.partial(kernel, n_blk, n_z, head ** -0.5),
-            out_shape=pltpu.VMEM((n_keys // 128, 128), f32),
+            out_shape=(pltpu.VMEM((n_keys // 128, 128), jnp.int16), pltpu.VMEM((2, 128), f32)),
             in_specs=[pl.BlockSpec(memory_space=pl.ANY)] * 4,
-            out_specs=pl.BlockSpec(memory_space=pltpu.VMEM),
+            out_specs=[pl.BlockSpec(memory_space=pltpu.VMEM)] * 2,
             scratch_shapes=[
                 pltpu.VMEM((rows, head), jnp.bfloat16),
                 pltpu.VMEM((n_keys, head), jnp.bfloat16),
@@ -327,15 +330,13 @@
                 pltpu.VMEM((PIECES, lines, 128), f32),
                 pltpu.VMEM((PIECES, n_z, lines, 128), f32),
                 pltpu.VMEM((PIECES, lines, 128), f32),
-                pltpu.VMEM((n_keys // 128, 128), jnp.int16),
-                pltpu.VMEM((2, 128), f32),
                 dma((4,)), dma((HALVES,)), dma((HALVES,)), dma, dma,
                 dma((PIECES,)), dma((PIECES,)), dma((PIECES,)), dma((2 * n_z,)), dma((2,)),
             ],
             compiler_params=pltpu.CompilerParams(
                 collective_id=0, has_side_effects=True, vmem_limit_bytes=16 * 1024 * 1024),
         )(*operands)
-        return out.reshape(n_keys)
+        return decode(code, bounds).reshape(n_keys)
 
     in_specs = (P(("blk", "qsub"), None), P("blk", None), P(("blk", "qsub")), P(("blk", "qsub")))
     return jax.shard_map(body, mesh=mesh, in_specs=in_specs, out_specs=P("blk"), check_vma=False)

time: 25.6 us -> 25.5 us (level)
  other arithmetic: 0 us -> 0.62 us
  local copies, waits for them, and re-layouts: 0.61 us -> 0.01 us
  Pallas kernels: 24.8 us -> 24.4 us
    reshape x0 -> x1, other arithmetic: none -> 0.62 us  [body(): return decode(code, bounds).reshape(n_keys)]
    unnamed x1 -> x0, local copies, waits for them, and re-layouts: 0.61 us -> none
    pallas_call x1, Pallas kernels: 24.8 us -> 24.4 us  [body(): pl.pallas_call(functools.partial(kernel, n_blk, n_z, head ** (-0.5)), out...]
where the time goes in v5:
time: 25.5 us; the launch traced here: 25.1 us
  Pallas kernels  24.4 us (96%)
  other arithmetic  0.62 us (2%)
    pallas_call x1, Pallas kernels, body(): pl.pallas_call(functools.partial(kernel, n_blk, n_z, head ** (-0.5)), out...  24.4 us
    reshape x1, other arithmetic, body(): return decode(code, bounds).reshape(n_keys)  0.62 us

profile of v5, /device:TPU:1, one launch (start us, length us, event | category | flops | bytes accessed | tf_op | source)
XLA Modules:
  0.0 25.1 jit_solution(18194726197223995605)
XLA Ops:
  0.0 24.4 %shard_map.46 = (s16[48,128]{1,0:T(8,128)(2,1)S(1)}, f32[2,128]{1,0:T(2,128)S(1)}) custom-call(bf16[384,128]{1,0:T(8,128)(2,1)} %q_hbm.1, bf16[6144,128]{1,0:T(8,128)(2,1)} %k_hbm.1, bf16[384]{0:T(512)(128)(2,1)} %ln_hbm.1, s32[384]{0:T(512)} %pos_hbm.1), custom_call_target="tpu_custom_call" | custom-call | tf_op jit(solution)/shard_map/pallas_call | solution.py:316
  24.5 0.6 %add_bitcast_fusion = f32[6144]{0:T(1024)} fusion(s16[48,128]{1,0:T(8,128)(2,1)S(1)} %get-tuple-element.7, f32[128]{0:T(128)S(1)} %get-tuple-element.10, f32[128]{0:T(128)S(1)} %get-tuple-element.9), kind=kLoop, calls=%fused_computation | loop fusion | flops 30720 | bytes 37888 | tf_op jit(solution)/shard_map/reshape | solution.py:339
  (1 shorter events, 0.0 us)

commit v6 on v5

--- a/solution.py
+++ b/solution.py
@@ -12,7 +12,8 @@
 FAR = 1e30
 TILE = 256
 HALVES = 2
-PIECES = 3
+PIECES = (2, 1)
+HOME = 3
 ROW = 8
 STEPS = 65000.0
 
@@ -67,9 +68,14 @@
     return dense(groups)
 
 
-def key_index(g, lines):
-    line = lax.broadcasted_iota(jnp.int32, (lines, 128), 0) + g * lines
+def key_index(first, lines):
+    line = lax.broadcasted_iota(jnp.int32, (lines, 128), 0) + first
     return line * 128 + lax.broadcasted_iota(jnp.int32, (lines, 128), 1)
+
+
+def cut(n_keys):
+    unit = n_keys // 128 // sum(PIECES)
+    return [(sum(PIECES[:g]) * unit, PIECES[g] * unit) for g in range(len(PIECES))]
 
 
 def encode(best):
@@ -88,7 +94,7 @@
     n_blk, n_z, scale,
     q_hbm, k_hbm, ln_hbm, pos_hbm, code_v, bound_v,
     q_v, k_v, ln_v, pos_v, qn_v, cs_v, cn_v,
-    home_v, part_v, recv_v, mid_v,
+    home_v, part_0, part_1, recv_0, recv_1, mid_0, mid_1,
     in_sem, qs_sem, qr_sem, cs_sem, cr_sem, rs_send, rs_early, rs_late, ag_send, ag_recv,
 ):
     b = lax.axis_index("blk")
@@ -96,8 +102,9 @@
     sends, n_late = plan(n_z)
     rows = q_v.shape[0]
     n_keys = k_v.shape[0]
-    width = n_keys // PIECES
-    lines = width // 128
+    cuts = list(enumerate(cut(n_keys)))
+    part_v, recv_v, mid_v = (part_0, part_1), (recv_0, recv_1), (mid_0, mid_1)
+    home_lines = n_keys // 128 // HOME
     part_rows = rows // HALVES
     before = lax.rem(b + n_blk - 1, n_blk)
     after = lax.rem(b + 1, n_blk)
@@ -174,10 +181,11 @@
 
     ins[3].wait()
     query = q_v[...]
-    for g in range(PIECES):
-        best = best_of(query, home_columns, k_v, g * width, width)
-        j = key_index(g, lines)
-        home_v[g * lines : (g + 1) * lines, :] = jnp.where((j >= low_home) & (j < start), best, NEG)
+    for g in range(HOME):
+        first = g * home_lines
+        best = best_of(query, home_columns, k_v, first * 128, home_lines * 128)
+        j = key_index(first, home_lines)
+        home_v[first : first + home_lines, :] = jnp.where((j >= low_home) & (j < start), best, NEG)
         if g == 0:
             pl.when(has_before & far)(send_queries)
 
@@ -206,19 +214,19 @@
     next_columns = down(cn[0:1, :])
     low_n = jnp.where(has_after, cn[1:2, 0:1], jnp.float32(4 * n_keys)).astype(jnp.int32)
 
-    def next_best(h, g):
+    def next_best(h, first, lines):
         some = next_columns[h * part_rows : (h + 1) * part_rows, :]
-        best = best_of(qn_v[h * part_rows : (h + 1) * part_rows, :], some, k_v, g * width, width)
+        best = best_of(qn_v[h * part_rows : (h + 1) * part_rows, :], some, k_v, first * 128, lines * 128)
         return jnp.maximum(
-            home_v[g * lines : (g + 1) * lines, :], jnp.where(key_index(g, lines) >= low_n, best, NEG))
+            home_v[first : first + lines, :], jnp.where(key_index(first, lines) >= low_n, best, NEG))
 
     for h in range(HALVES - 1):
         @pl.when(has_after)
         def _():
             send_q[h].wait_recv()
 
-        for g in range(PIECES):
-            home_v[g * lines : (g + 1) * lines, :] = next_best(h, g)
+        for _, (first, lines) in cuts:
+            home_v[first : first + lines, :] = next_best(h, first, lines)
 
     @pl.when(has_after)
     def _():
@@ -226,7 +234,7 @@
 
     def reduce_copy(g, sem):
         return pltpu.make_async_remote_copy(
-            src_ref=part_v.at[g], dst_ref=recv_v.at[g, slot], send_sem=rs_send.at[g], recv_sem=sem.at[g],
+            src_ref=part_v[g], dst_ref=recv_v[g].at[slot], send_sem=rs_send.at[g], recv_sem=sem.at[g],
             device_id={"qsub": 0}, device_id_type=MESH)
 
     def give(p, at):
@@ -247,17 +255,17 @@
 
     @pl.when(z == 0)
     def _():
-        for g in range(PIECES):
-            recv_v[g, turn] = next_best(HALVES - 1, g)
-        for g in range(PIECES):
-            arrived = recv_v.at[g, pl.ds(0, first_late - 1)]
+        for g, (first, lines) in cuts:
+            recv_v[g][turn] = next_best(HALVES - 1, first, lines)
+        for g, _ in cuts:
+            arrived = recv_v[g].at[pl.ds(0, first_late - 1)]
             pltpu.make_async_copy(arrived, arrived, rs_early.at[g]).wait()
-            mid_v[g] = jnp.max(recv_v[g, 0:first_late], axis=0)
+            mid_v[g][...] = jnp.max(recv_v[g][0:first_late], axis=0)
         full = []
-        for g in range(PIECES):
-            arrived = recv_v.at[g, pl.ds(first_late, n_late)]
+        for g, _ in cuts:
+            arrived = recv_v[g].at[pl.ds(first_late, n_late)]
             pltpu.make_async_copy(arrived, arrived, rs_late.at[g]).wait()
-            full.append(jnp.maximum(mid_v[g], jnp.max(recv_v[g, first_late:n_z], axis=0)) * scale)
+            full.append(jnp.maximum(mid_v[g][...], jnp.max(recv_v[g][first_late:n_z], axis=0)) * scale)
         code, bounds = encode(jnp.concatenate(full, axis=0))
         code_v[...] = code
         bound_v[...] = bounds
@@ -269,8 +277,8 @@
             pl.semaphore_wait(barrier, 1)
 
         late = (z >= n_z // 2) & (z < n_z // 2 + n_late)
-        for g in range(PIECES):
-            part_v[g] = next_best(HALVES - 1, g)
+        for g, (first, lines) in cuts:
+            part_v[g][...] = next_best(HALVES - 1, first, lines)
 
             @pl.when(late)
             def _():
@@ -291,7 +299,7 @@
 
     @pl.when(z != 0)
     def _():
-        for g in range(PIECES):
+        for g, _ in cuts:
             reduce_copy(g, rs_early).wait_send()
 
     @pl.when(has_before)
@@ -307,7 +315,7 @@
     def body(queries, key_rows, log_norms, positions):
         rows, head = queries.shape
         n_keys = key_rows.shape[0]
-        lines = n_keys // PIECES // 128
+        pieces = [lines for _, lines in cut(n_keys)]
         f32 = jnp.float32
         dma = pltpu.SemaphoreType.DMA
         operands = [
@@ -327,11 +335,11 @@
                 pltpu.VMEM((2, rows), f32),
                 pltpu.VMEM((2, rows), f32),
                 pltpu.VMEM((n_keys // 128, 128), f32),
-                pltpu.VMEM((PIECES, lines, 128), f32),
-                pltpu.VMEM((PIECES, n_z, lines, 128), f32),
-                pltpu.VMEM((PIECES, lines, 128), f32),
+                *[pltpu.VMEM((lines, 128), f32) for lines in pieces],
+                *[pltpu.VMEM((n_z, lines, 128), f32) for lines in pieces],
+                *[pltpu.VMEM((lines, 128), f32) for lines in pieces],
                 dma((4,)), dma((HALVES,)), dma((HALVES,)), dma, dma,
-                dma((PIECES,)), dma((PIECES,)), dma((PIECES,)), dma((2 * n_z,)), dma((2,)),
+                dma((len(pieces),)), dma((len(pieces),)), dma((len(pieces),)), dma((2 * n_z,)), dma((2,)),
             ],
             compiler_params=pltpu.CompilerParams(
                 collective_id=0, has_side_effects=True, vmem_limit_bytes=16 * 1024 * 1024),

time: 25.5 us -> 25.4 us (level)
  the two profiles are of different devices: /device:TPU:1 before, /device:TPU:184 now
where the time goes in v6:
time: 25.4 us; the launch traced here: 25.3 us
  Pallas kernels  24.7 us (97%)
  other arithmetic  0.62 us (2%)
    pallas_call x1, Pallas kernels, body(): pl.pallas_call(functools.partial(kernel, n_blk, n_z, head ** (-0.5)), out...  24.7 us
    reshape x1, other arithmetic, body(): return decode(code, bounds).reshape(n_keys)  0.62 us

profile of v6, /device:TPU:184, one launch (start us, length us, event | category | flops | bytes accessed | tf_op | source)
XLA Modules:
  0.0 25.3 jit_solution(5767238092370241078)
XLA Ops:
  0.0 24.7 %shard_map.46 = (s16[48,128]{1,0:T(8,128)(2,1)S(1)}, f32[2,128]{1,0:T(2,128)S(1)}) custom-call(bf16[384,128]{1,0:T(8,128)(2,1)} %q_hbm.1, bf16[6144,128]{1,0:T(8,128)(2,1)} %k_hbm.1, bf16[384]{0:T(512)(128)(2,1)} %ln_hbm.1, s32[384]{0:T(512)} %pos_hbm.1), custom_call_target="tpu_custom_call" | custom-call | tf_op jit(solution)/shard_map/pallas_call | solution.py:324
  24.7 0.6 %add_bitcast_fusion = f32[6144]{0:T(1024)} fusion(s16[48,128]{1,0:T(8,128)(2,1)S(1)} %get-tuple-element.7, f32[128]{0:T(128)S(1)} %get-tuple-element.10, f32[128]{0:T(128)S(1)} %get-tuple-element.9), kind=kLoop, calls=%fused_computation | loop fusion | flops 30720 | bytes 37888 | tf_op jit(solution)/shard_map/reshape | solution.py:347
  (1 shorter events, 0.0 us)

commit v7 on v6

--- a/solution.py
+++ b/solution.py
@@ -20,8 +20,10 @@
 
 def plan(n_z):
     if n_z == 16:
-        return {0: [1, 4, 2, 15, 3], 4: [5, 6, 7], 15: [8, 9, 10, 11, 12, 13, 14]}, 4
-    return {0: list(range(1, n_z))}, 1
+        last = [8, 9, 10, 11, 12, 13, 14]
+        even = {0: [1, 4, 2, 5, 3, 15], 4: [6], 5: [7], 15: last}
+        return (even, {0: [1, 4, 2, 15, 3], 4: [5, 6, 7], 15: last}), 4
+    return ({0: list(range(1, n_z))},) * 2, 1
 
 
 def dot_rows(left, right):
@@ -245,8 +247,8 @@
             for i, ref in enumerate((bound_v, code_v))
         ]
 
-    def pass_on(source, done):
-        for at, p in enumerate(sends[source]):
+    def pass_on(targets, done):
+        for at, p in enumerate(targets):
             for copy in give(p, at):
                 if done:
                     copy.wait_send()
@@ -291,11 +293,16 @@
         for copy in give(0, 0):
             copy.wait_recv()
 
-    for source in sends:
-        pl.when(z == source)(functools.partial(pass_on, source, False))
-
-    for source in sends:
-        pl.when(z == source)(functools.partial(pass_on, source, True))
+    givers = [
+        ((z == source) & (lax.rem(b, 2) == odd), targets)
+        for odd in range(2)
+        for source, targets in sends[odd].items()
+    ]
+    for gives, targets in givers:
+        pl.when(gives)(functools.partial(pass_on, targets, False))
+
+    for gives, targets in givers:
+        pl.when(gives)(functools.partial(pass_on, targets, True))
 
     @pl.when(z != 0)
     def _():

time: 25.4 us -> 25.3 us (level)
  the two profiles are of different devices: /device:TPU:184 before, /device:TPU:1 now
where the time goes in v7:
time: 25.3 us; the launch traced here: 24.9 us
  Pallas kernels  24.3 us (96%)
  other arithmetic  0.62 us (2%)
    pallas_call x1, Pallas kernels, body(): pl.pallas_call(functools.partial(kernel, n_blk, n_z, head ** (-0.5)), out...  24.3 us
    reshape x1, other arithmetic, body(): return decode(code, bounds).reshape(n_keys)  0.62 us

profile of v7, /device:TPU:1, one launch (start us, length us, event | category | flops | bytes accessed | tf_op | source)
XLA Modules:
  0.0 24.9 jit_solution(4327415064736572279)
XLA Ops:
  0.0 24.3 %shard_map.46 = (s16[48,128]{1,0:T(8,128)(2,1)S(1)}, f32[2,128]{1,0:T(2,128)S(1)}) custom-call(bf16[384,128]{1,0:T(8,128)(2,1)} %q_hbm.1, bf16[6144,128]{1,0:T(8,128)(2,1)} %k_hbm.1, bf16[384]{0:T(512)(128)(2,1)} %ln_hbm.1, s32[384]{0:T(512)} %pos_hbm.1), custom_call_target="tpu_custom_call" | custom-call | tf_op jit(solution)/shard_map/pallas_call | solution.py:331
  24.3 0.6 %add_bitcast_fusion = f32[6144]{0:T(1024)} fusion(s16[48,128]{1,0:T(8,128)(2,1)S(1)} %get-tuple-element.7, f32[128]{0:T(128)S(1)} %get-tuple-element.10, f32[128]{0:T(128)S(1)} %get-tuple-element.9), kind=kLoop, calls=%fused_computation | loop fusion | flops 30720 | bytes 37888 | tf_op jit(solution)/shard_map/reshape | solution.py:354
  (1 shorter events, 0.0 us)

commit v8 on v7

--- a/solution.py
+++ b/solution.py
@@ -97,7 +97,7 @@
     q_hbm, k_hbm, ln_hbm, pos_hbm, code_v, bound_v,
     q_v, k_v, ln_v, pos_v, qn_v, cs_v, cn_v,
     home_v, part_0, part_1, recv_0, recv_1, mid_0, mid_1,
-    in_sem, qs_sem, qr_sem, cs_sem, cr_sem, rs_send, rs_early, rs_late, ag_send, ag_recv,
+    in_sem, qs_sem, qr_sem, cs_sem, cr_sem, rs_send, rs_recv, ag_send, ag_recv,
 ):
     b = lax.axis_index("blk")
     z = lax.axis_index("qsub")
@@ -234,9 +234,11 @@
     def _():
         send_q[HALVES - 1].wait_recv()
 
-    def reduce_copy(g, sem):
+    group = ((z >= n_z // 2) & (z < n_z // 2 + n_late)).astype(jnp.int32)
+
+    def reduce_copy(g):
         return pltpu.make_async_remote_copy(
-            src_ref=part_v[g], dst_ref=recv_v[g].at[slot], send_sem=rs_send.at[g], recv_sem=sem.at[g],
+            src_ref=part_v[g], dst_ref=recv_v[g].at[slot], send_sem=rs_send.at[g], recv_sem=rs_recv.at[group * len(cuts) + g],
             device_id={"qsub": 0}, device_id_type=MESH)
 
     def give(p, at):
@@ -261,12 +263,12 @@
             recv_v[g][turn] = next_best(HALVES - 1, first, lines)
         for g, _ in cuts:
             arrived = recv_v[g].at[pl.ds(0, first_late - 1)]
-            pltpu.make_async_copy(arrived, arrived, rs_early.at[g]).wait()
+            pltpu.make_async_copy(arrived, arrived, rs_recv.at[g]).wait()
             mid_v[g][...] = jnp.max(recv_v[g][0:first_late], axis=0)
         full = []
         for g, _ in cuts:
             arrived = recv_v[g].at[pl.ds(first_late, n_late)]
-            pltpu.make_async_copy(arrived, arrived, rs_late.at[g]).wait()
+            pltpu.make_async_copy(arrived, arrived, rs_recv.at[len(cuts) + g]).wait()
             full.append(jnp.maximum(mid_v[g][...], jnp.max(recv_v[g][first_late:n_z], axis=0)) * scale)
         code, bounds = encode(jnp.concatenate(full, axis=0))
         code_v[...] = code
@@ -278,17 +280,9 @@
         def _():
             pl.semaphore_wait(barrier, 1)
 
-        late = (z >= n_z // 2) & (z < n_z // 2 + n_late)
         for g, (first, lines) in cuts:
             part_v[g][...] = next_best(HALVES - 1, first, lines)
-
-            @pl.when(late)
-            def _():
-                reduce_copy(g, rs_late).start()
-
-            @pl.when(jnp.logical_not(late))
-            def _():
-                reduce_copy(g, rs_early).start()
+            reduce_copy(g).start()
 
         for copy in give(0, 0):
             copy.wait_recv()
@@ -307,7 +301,7 @@
     @pl.when(z != 0)
     def _():
         for g, _ in cuts:
-            reduce_copy(g, rs_early).wait_send()
+            reduce_copy(g).wait_send()
 
     @pl.when(has_before)
     def _():
@@ -346,7 +340,7 @@
                 *[pltpu.VMEM((n_z, lines, 128), f32) for lines in pieces],
                 *[pltpu.VMEM((lines, 128), f32) for lines in pieces],
                 dma((4,)), dma((HALVES,)), dma((HALVES,)), dma, dma,
-                dma((len(pieces),)), dma((len(pieces),)), dma((len(pieces),)), dma((2 * n_z,)), dma((2,)),
+                dma((len(pieces),)), dma((2 * len(pieces),)), dma((2 * n_z,)), dma((2,)),
             ],
             compiler_params=pltpu.CompilerParams(
                 collective_id=0, has_side_effects=True, vmem_limit_bytes=16 * 1024 * 1024),

time: 25.3 us -> 25.3 us (level)
  no operation moved by 1% of the time
where the time goes in v8:
time: 25.3 us; the launch traced here: 24.9 us
  Pallas kernels  24.3 us (96%)
  other arithmetic  0.62 us (2%)
    pallas_call x1, Pallas kernels, body(): pl.pallas_call(functools.partial(kernel, n_blk, n_z, head ** (-0.5)), out...  24.3 us
    reshape x1, other arithmetic, body(): return decode(code, bounds).reshape(n_keys)  0.62 us

profile of v8, /device:TPU:1, one launch (start us, length us, event | category | flops | bytes accessed | tf_op | source)
XLA Modules:
  0.0 24.9 jit_solution(11127709995476658109)
XLA Ops:
  0.0 24.3 %shard_map.46 = (s16[48,128]{1,0:T(8,128)(2,1)S(1)}, f32[2,128]{1,0:T(2,128)S(1)}) custom-call(bf16[384,128]{1,0:T(8,128)(2,1)} %q_hbm.1, bf16[6144,128]{1,0:T(8,128)(2,1)} %k_hbm.1, bf16[384]{0:T(512)(128)(2,1)} %ln_hbm.1, s32[384]{0:T(512)} %pos_hbm.1), custom_call_target="tpu_custom_call" | custom-call | tf_op jit(solution)/shard_map/pallas_call | solution.py:325
  24.3 0.6 %add_bitcast_fusion = f32[6144]{0:T(1024)} fusion(s16[48,128]{1,0:T(8,128)(2,1)S(1)} %get-tuple-element.7, f32[128]{0:T(128)S(1)} %get-tuple-element.10, f32[128]{0:T(128)S(1)} %get-tuple-element.9), kind=kLoop, calls=%fused_computation | loop fusion | flops 30720 | bytes 37888 | tf_op jit(solution)/shard_map/reshape | solution.py:348
  (1 shorter events, 0.0 us)

commit v9 on v8

--- a/solution.py
+++ b/solution.py
@@ -222,6 +222,10 @@
         return jnp.maximum(
             home_v[first : first + lines, :], jnp.where(key_index(first, lines) >= low_n, best, NEG))
 
+    @pl.when(jnp.logical_not(has_before) & (z != 0))
+    def _():
+        pl.semaphore_wait(barrier, 1)
+
     for h in range(HALVES - 1):
         @pl.when(has_after)
         def _():
@@ -276,10 +280,6 @@
 
     @pl.when(z != 0)
     def _():
-        @pl.when(jnp.logical_not(has_before))
-        def _():
-            pl.semaphore_wait(barrier, 1)
-
         for g, (first, lines) in cuts:
             part_v[g][...] = next_best(HALVES - 1, first, lines)
             reduce_copy(g).start()

time: 25.3 us -> 25.3 us (level)
  no operation moved by 1% of the time
where the time goes in v9:
time: 25.3 us; the launch traced here: 24.9 us
  Pallas kernels  24.3 us (96%)
  other arithmetic  0.62 us (2%)
    pallas_call x1, Pallas kernels, body(): pl.pallas_call(functools.partial(kernel, n_blk, n_z, head ** (-0.5)), out...  24.3 us
    reshape x1, other arithmetic, body(): return decode(code, bounds).reshape(n_keys)  0.62 us

profile of v9, /device:TPU:1, one launch (start us, length us, event | category | flops | bytes accessed | tf_op | source)
XLA Modules:
  0.0 24.9 jit_solution(10374364112827720280)
XLA Ops:
  0.0 24.3 %shard_map.46 = (s16[48,128]{1,0:T(8,128)(2,1)S(1)}, f32[2,128]{1,0:T(2,128)S(1)}) custom-call(bf16[384,128]{1,0:T(8,128)(2,1)} %q_hbm.1, bf16[6144,128]{1,0:T(8,128)(2,1)} %k_hbm.1, bf16[384]{0:T(512)(128)(2,1)} %ln_hbm.1, s32[384]{0:T(512)} %pos_hbm.1), custom_call_target="tpu_custom_call" | custom-call | tf_op jit(solution)/shard_map/pallas_call | solution.py:325
  24.3 0.6 %add_bitcast_fusion = f32[6144]{0:T(1024)} fusion(s16[48,128]{1,0:T(8,128)(2,1)S(1)} %get-tuple-element.7, f32[128]{0:T(128)S(1)} %get-tuple-element.10, f32[128]{0:T(128)S(1)} %get-tuple-element.9), kind=kLoop, calls=%fused_computation | loop fusion | flops 30720 | bytes 37888 | tf_op jit(solution)/shard_map/reshape | solution.py:348
  (1 shorter events, 0.0 us)
